TPU v7x, 32 devices: a whole 2x2x4 slice. The times are simulated.
32 devices in a mesh: band: 2 (over x), stn: 8 (over z, y), tm: 2 (over core).
Axes of the slice: x: 2, y: 2, z: 4, core: 2. Of those that a mesh axis runs over, the one named last changes fastest.
Arguments:
- voltages: int32 [704, 4, 32768], P('stn', 'band', 'tm'), parts along dimension 1, may hold values from -125 to 125, as said below
- filter_taps: float32 [16, 128], replicated, may hold values from -0.036 to 0.036
Outputs:
- visibilities: float32 [2, 2, 128, 704, 704], P(None, None, ('band', 'stn', 'tm')), parts along dimension 2
There are 2 independent parts, one for each index of `band`. A program takes and returns all parts, laid end to end along the dimension named above; an argument that names none is the same for every part. Nothing has to cross between parts.
Inputs may be any that keep to these rules, and one draw needn't show every extreme that they name: `voltages`: each input's samples are an integer gain of -2 to 2 times a signal common to all inputs plus noise of its own.
All inputs are finite; a program needn't handle non-finite values.
Results may differ from a plain program's by a relative error of at most 0.00049.
Values may be sent and summed in bfloat16 or wider, within the bound.
A program may use at most 192 MiB of HBM per device.

v0:
```python
import math
import jax
import jax.numpy as jnp
from jax import lax
from jax.sharding import PartitionSpec as P


def passed_along(value, axis, steps):
    count = lax.axis_size(axis)
    pairs = [(source, (source + steps) % count) for source in range(count)]
    return lax.ppermute(value, axis, pairs)


def transform_table(frame_len, chan_count):
    sample_index = jnp.arange(frame_len, dtype=jnp.int32)[:, None]
    chan_index = jnp.arange(chan_count, dtype=jnp.int32)[None, :]
    phase = (2 * chan_index + 1) * sample_index % (2 * frame_len)
    angle = phase.astype(jnp.float32) * (math.pi / frame_len)
    factor = 1.0 / math.sqrt(frame_len)
    cosine = jnp.cos(angle) * factor
    sine = -jnp.sin(angle) * factor
    return jnp.stack([cosine, sine], axis=2).reshape(frame_len, 2 * chan_count)


def arrange(blocks):
    stations, blocks_time, per_dev, parts_two, inputs_dev, sub_count, spec_dev = blocks.shape
    ordered = jnp.transpose(blocks, (3, 5, 2, 0, 4, 1, 6))
    return ordered.reshape(
        parts_two, sub_count, per_dev, stations * inputs_dev, blocks_time * spec_dev
    )


def correlate(stacked):
    real_in = stacked[0]
    imag_in = stacked[1]
    right_side = jnp.concatenate([real_in, imag_in], axis=-1)
    left_imag = jnp.concatenate([imag_in, -real_in], axis=-1)
    real_part = jnp.einsum(
        "gcis,gcjs->gcij", right_side, right_side, preferred_element_type=jnp.float32
    )
    imag_part = jnp.einsum(
        "gcis,gcjs->gcij", left_imag, right_side, preferred_element_type=jnp.float32
    )
    return jnp.stack([real_part, imag_part])


def shards(voltages, filter_taps):
    inputs_dev, sub_count, time_dev = voltages.shape
    taps_count, frame_len = filter_taps.shape
    spec_dev = time_dev // frame_len
    chan_count = frame_len // 2
    lagging = taps_count - 1
    frames = voltages.astype(jnp.bfloat16).reshape(inputs_dev, sub_count, spec_dev, frame_len)
    last_frames = frames[:, :, spec_dev - lagging :, :]
    received = passed_along(last_frames, "tm", 1)
    earlier = jnp.concatenate([jnp.zeros_like(received[:, :1]), received[:, :-1]], axis=1)
    history = jnp.where(lax.axis_index("tm") == 0, earlier, received)
    extended = jnp.concatenate([history, frames], axis=2).astype(jnp.float32)
    filtered = filter_taps[0] * extended[:, :, 0:spec_dev]
    for tap_index in range(1, taps_count):
        filtered = (
            filtered + filter_taps[tap_index] * extended[:, :, tap_index : tap_index + spec_dev]
        )
    table = transform_table(frame_len, chan_count)
    spectra = lax.dot_general(
        table,
        filtered.reshape(-1, frame_len),
        (((0,), (1,)), ((), ())),
        precision=lax.Precision.HIGHEST,
        preferred_element_type=jnp.float32,
    ).astype(jnp.bfloat16)
    stations = lax.axis_size("stn")
    halves = lax.axis_size("tm")
    scale = 1.0 / (spec_dev * halves)
    moved = lax.all_to_all(spectra[None], ("stn", "tm"), split_axis=1, concat_axis=0, tiled=True)
    per_dev = moved.shape[1] // 2
    blocks = moved.reshape(stations, halves, per_dev, 2, inputs_dev, sub_count, spec_dev)
    result = correlate(arrange(blocks))
    return result * scale


def solution(mesh):
    placed = (P("stn", "band", "tm"), P())
    return jax.shard_map(
        shards,
        mesh=mesh,
        in_specs=placed,
        out_specs=P(None, None, ("band", "stn", "tm"), None, None),
        check_vma=False,
    )
```

profile of v0, /device:TPU:1, one launch (start us, length us, event | category | flops | bytes accessed | tf_op | source)
XLA Modules:
  0.0 507.7 jit_solution(10586503539075918280)
XLA Ops:
  0.0 9.0 %convert_element_type.26 = bf16[88,2,16384]{2,1,0:T(2,128)(2,1)} convert(s32[88,2,16384]{2,1,0:T(2,128)} %param.2) | non-fusion elementwise | flops 2883584 | bytes 17301504 | tf_op jit(solution)/shard_map/convert_element_type | solution.py:53
  9.0 0.0 copy-start.1
  9.0 10.5 %reshape.154 = bf16[88,2,128,128]{3,2,1,0:T(8,128)(2,1)} reshape(bf16[88,2,16384]{2,1,0:T(2,128)(2,1)} %convert_element_type.26) | data formatting | bytes 11534336 | tf_op jit(solution)/shard_map/reshape | solution.py:53
  19.5 1.4 slice.146
  20.9 0.1 copy.33
  21.1 0.2 copy.19
  21.3 0.1 collective-permute-start
  21.4 0.2 cosine_multiply_fusion
  21.6 0.1 copy.17
  21.7 0.0 copy-done.1
  21.7 1.7 collective-permute-done
  23.5 0.1 copy.28
  23.6 0.2 pad_select_fusion
  23.7 10.6 %maximum_convert_fusion = f32[88,2,143,128]{3,2,0,1:T(8,128)} fusion(bf16[88,2,15,128]{3,2,0,1:T(8,128)(2,1)S(1)} %pad_select_fusion, bf16[88,2,128,128]{3,2,1,0:T(8,128)(2,1)} %reshape.154), kind=kLoop, calls=%fused_computation.36 | loop fusion | flops 12886016 | bytes 19329024 | tf_op jit(solution)/shard_map/convert_element_type | solution.py:58
  34.3 74.6 %fusion.1 = f32[88,2,128,128]{3,2,0,1:T(8,128)} fusion(f32[88,2,143,128]{3,2,0,1:T(8,128)} %maximum_convert_fusion, f32[128]{0:T(128)S(1)} %get-tuple-element.23, f32[128]{0:T(128)S(1)} %get-tuple-element.24, f32[128]{0:T(128)S(1)} %get-tuple-element.10, f32[128]{0:T(128)S(1)} %get-tuple-element.11, f32[128]{0:T(128)S(1)} %get-tuple-element.12, ...), kind=kLoop, calls=%fused_computation.4 | loop fusion | flops 89391104 | bytes 196091904 | tf_op jit(solution)/shard_map/add | solution.py:62
  109.0 10.6 %copy.22 = f32[88,2,128,128]{3,2,1,0:T(8,128)} copy(f32[88,2,128,128]{3,2,0,1:T(8,128)} %fusion.1) | data formatting | bytes 23068672 | tf_op jit(solution)/shard_map/add | solution.py:62
  119.6 13.6 %fusion = bf16[1,128,22528]{2,1,0:T(8,128)(2,1)S(1)} fusion(f32[128,128]{0,1:T(8,128)S(1)} %bitcast.54, f32[22528,128]{1,0:T(8,128)} %bitcast.52), kind=kOutput, calls=%fused_computation.2 | convolution fusion | flops 4432068608 | bytes 17367040 | tf_op jit(solution)/shard_map/dot_general | solution.py:65
  133.2 47.5 %copy.32 = bf16[1,128,22528]{2,0,1:T(2,128)(2,1)} copy(bf16[1,128,22528]{2,1,0:T(8,128)(2,1)S(1)} %fusion) | data formatting | bytes 11534336 | tf_op jit(solution)/shard_map/broadcast_in_dim | solution.py:75
  180.7 0.6 broadcast.142
  181.3 35.9 %reduce.2 = bf16[128,22528]{1,0:T(8,128)(2,1)} reduce(bf16[128,1,22528]{2,1,0:T(2,128)(2,1)} %bitcast.51, bf16[]{:T(256)} %broadcast.142), dimensions={1}, to_apply=%bitcast.50.reduce_sub_computation | reduce | bytes 11534338
  217.2 13.4 %reshape.156 = bf16[16,2,90112]{2,1,0:T(2,128)(2,1)} reshape(bf16[128,22528]{1,0:T(8,128)(2,1)} %reduce.2) | data formatting | bytes 11534336
  230.5 133.9 %all_to_all.4 = bf16[16,2,90112]{2,1,0:T(2,128)(2,1)} all-to-all(bf16[16,2,90112]{2,1,0:T(2,128)(2,1)} %reshape.156), channel_id=1, replica_groups=mesh['band'=2,'stn'=8,'tm'=2] {'stn','tm'}, dimensions={0} | all-to-all | bytes 11534336 | tf_op jit(solution)/shard_map/all_to_all | solution.py:75
  364.5 13.8 %reshape.157 = bf16[128,1,22528]{2,1,0:T(2,128)(2,1)} reshape(bf16[16,2,90112]{2,1,0:T(2,128)(2,1)} %all_to_all.4) | data formatting | bytes 11534336
  378.3 36.0 %bitcast_reduce_fusion = bf16[128,22528]{1,0:T(8,128)(2,1)} fusion(bf16[128,1,22528]{2,1,0:T(2,128)(2,1)} %reshape.157), kind=kLoop, calls=%fused_computation.75 | loop fusion | bytes 11534336 | tf_op jit(solution)/shard_map/all_to_all | solution.py:75
  414.3 8.9 %reshape.153 = bf16[8,2,4,2,88,2,128]{6,5,4,3,2,1,0:T(2,128)(2,1)} reshape(bf16[128,22528]{1,0:T(8,128)(2,1)} %bitcast_reduce_fusion) | data formatting | bytes 11534336 | tf_op jit(solution)/shard_map/reshape | solution.py:77
  423.2 8.4 %fusion.26 = (bf16[1,2,4,8,88,2,128]{6,1,4,0,2,5,3:T(2,128)(2,1)S(1)}, bf16[1,2,4,8,88,2,128]{6,1,4,0,2,5,3:T(2,128)(2,1)}) fusion(bf16[2,2,4,8,88,2,128]{6,1,4,0,2,5,3:T(2,128)(2,1)} %bitcast.53), kind=kLoop, calls=%fused_computation.73 | loop fusion | bytes 11534336 | tf_op jit(solution)/shard_map/slice | solution.py:35
  431.7 4.5 copy.25
  436.2 6.5 %squeeze.7 = bf16[2,4,704,256]{3,2,1,0:T(8,128)(2,1)S(1)} reshape(bf16[1,2,4,8,88,2,128]{6,5,4,3,2,1,0:T(2,128)(2,1)} %copy.25) | data formatting | bytes 5767168 | tf_op jit(solution)/shard_map/squeeze | solution.py:35
  442.8 6.4 %copy.24 = bf16[1,2,4,8,88,2,128]{6,5,4,3,2,1,0:T(2,128)(2,1)} copy(bf16[1,2,4,8,88,2,128]{6,1,4,0,2,5,3:T(2,128)(2,1)} %get-tuple-element.6) | data formatting | bytes 5767168 | tf_op jit(solution)/shard_map/slice | solution.py:34
  449.1 7.4 %squeeze.6 = bf16[2,4,704,256]{3,2,1,0:T(8,128)(2,1)} reshape(bf16[1,2,4,8,88,2,128]{6,5,4,3,2,1,0:T(2,128)(2,1)} %copy.24) | data formatting | bytes 5767168 | tf_op jit(solution)/shard_map/squeeze | solution.py:34
  456.6 5.0 fusion.27
  461.6 0.2 constant_dynamic-update-slice_fusion
  461.8 0.0 copy-start
  461.9 8.4 %convolution_bitcast_fusion.1 = f32[1,2,4,704,704]{4,3,2,1,0:T(8,128)} fusion(bf16[2,4,704,512]{3,2,1,0:T(8,128)(2,1)S(1)} %constant_dynamic-update-slice_fusion), kind=kOutput, calls=%fused_computation.35 | convolution fusion | flops 4060086272 | bytes 21626880 | tf_op jit(solution)/shard_map/gcis,gcjs->gcij/dot_general | solution.py:38
  470.3 0.0 copy-done
  470.3 14.1 %convolution_bitcast_fusion = f32[1,2,4,704,704]{4,3,2,1,0:T(8,128)} fusion(bf16[2,4,704,512]{3,2,1,0:T(8,128)(2,1)} %copy-done, bf16[2,4,704,256]{3,2,1,0:T(8,128)(2,1)} %get-tuple-element.7, bf16[2,4,704,256]{3,2,1,0:T(8,128)(2,1)S(1)} %squeeze.7), kind=kOutput, calls=%fused_computation.34 | convolution fusion | flops 4071620608 | bytes 27394048 | tf_op jit(solution)/shard_map/gcis,gcjs->gcij/dot_general | solution.py:41
  484.4 23.2 %maximum_multiply_fusion = f32[2,2,4,704,704]{4,3,2,1,0:T(8,128)} fusion(f32[1,2,4,704,704]{4,3,2,1,0:T(8,128)} %convolution_bitcast_fusion, f32[1,2,4,704,704]{4,3,2,1,0:T(8,128)} %convolution_bitcast_fusion.1), kind=kLoop, calls=%fused_computation | loop fusion | flops 15859712 | bytes 63438848 | tf_op jit(solution)/shard_map/mul | solution.py:79
  (4 shorter events, 0.0 us)
Async XLA Ops:
  9.0 12.7 %copy-start.1 = (f32[16,128]{1,0:T(8,128)S(1)}, f32[16,128]{1,0:T(8,128)}, u32[]{:S(2)}) copy-start(f32[16,128]{1,0:T(8,128)} %param.3) | copy-start | bytes 24580
  21.3 2.2 collective-permute-start
  461.8 8.4 %copy-start = (bf16[2,4,704,512]{3,2,1,0:T(8,128)(2,1)}, bf16[2,4,704,512]{3,2,1,0:T(8,128)(2,1)S(1)}, u32[]{:S(2)}) copy-start(bf16[2,4,704,512]{3,2,1,0:T(8,128)(2,1)S(1)} %constant_dynamic-update-slice_fusion) | copy-start | bytes 17301508
where the time goes:
time: 516 us; the launch traced here: 508 us
  local copies, waits for them, and re-layouts  177 us (34%)
  other arithmetic  159 us (31%)
  blocking collectives  134 us (26%)
  matrix products  36.1 us (7%)
    all_to_all x1, blocking collectives, shards(): lax.all_to_all(spectra[None], ('stn', 'tm'), split_axis=1, concat_axis=0,...  134 us
    add x1, other arithmetic, shards(): filtered + filter_taps[tap_index] * extended[:, :, tap_index:tap_index +...  74.6 us
    broadcast_in_dim x1, local copies, waits for them, and re-layouts, shards(): spectra[None]  47.5 us
    all_to_all x1, local copies, waits for them, and re-layouts, shards(): lax.all_to_all(spectra[None], ('stn', 'tm'), split_axis=1, concat_axis=0,...  36 us
    unnamed x1, other arithmetic  35.9 us
    unnamed x9, local copies, waits for them, and re-layouts  28 us
    mul x1, other arithmetic, shards(): return result * scale  23.2 us
    dot_general x1, matrix products, correlate(): jnp.einsum('gcis,gcjs->gcij', left_imag, right_side, preferred_element_ty...  14.1 us
  transfers between devices with their start and end apart: 1, of which 1 were waited for; matrix products, arithmetic and copies ran while one was open for 0% of the time, Pallas kernels for 0%

commit v1 on v0

--- a/solution.py
+++ b/solution.py
@@ -3,6 +3,29 @@
 import jax.numpy as jnp
 from jax import lax
 from jax.sharding import PartitionSpec as P
+
+
+def split_up(shard, dim, size):
+    shape = shard.shape
+    parts = shard.reshape(*shape[:dim], size, shape[dim] // size, *shape[dim + 1 :])
+    return jnp.moveaxis(parts, dim, 0)
+
+
+def in_order(blocks, dim):
+    blocks = jnp.moveaxis(blocks, 0, dim)
+    dims = blocks.shape
+    return blocks.reshape(*dims[:dim], dims[dim] * dims[dim + 1], *dims[dim + 2 :])
+
+
+def swapped_with_each(array, axis, split_dim, concat_dim):
+    size, index = (lax.axis_size(axis), lax.axis_index(axis))
+    tiles = split_up(array, split_dim, size)
+    gathered = [tiles[index]]
+    for turn in range(1, size):
+        sent = tiles[index ^ turn]
+        gathered.append(lax.ppermute(sent, axis, [(i, i ^ turn) for i in range(size)]))
+    tiles = jnp.stack(gathered)[index ^ jnp.arange(size)]
+    return in_order(tiles, concat_dim)
 
 
 def passed_along(value, axis, steps):
@@ -72,7 +95,7 @@
     stations = lax.axis_size("stn")
     halves = lax.axis_size("tm")
     scale = 1.0 / (spec_dev * halves)
-    moved = lax.all_to_all(spectra[None], ("stn", "tm"), split_axis=1, concat_axis=0, tiled=True)
+    moved = swapped_with_each(spectra[None], ("stn", "tm"), 1, 0)
     per_dev = moved.shape[1] // 2
     blocks = moved.reshape(stations, halves, per_dev, 2, inputs_dev, sub_count, spec_dev)
     result = correlate(arrange(blocks))

time: 516 us -> 396 us (0.77); the launches traced: 508 us -> 394 us
  blocking collectives: 134 us -> 0 us
  waiting for transfers between devices: 1.73 us -> 129 us
  local copies, waits for them, and re-layouts: 177 us -> 83.8 us
  other arithmetic: 159 us -> 123 us
  starting transfers between devices: 0.12 us -> 22.1 us
    all_to_all x1 -> x0, blocking collectives: 134 us -> none  [shards(): lax.all_to_all(spectra[None], ('stn', 'tm'), split_axis=1, concat_axis=0,...]
    ppermute x0 -> x15, waiting for transfers between devices: none -> 127 us  [swapped_with_each(): lax.ppermute(sent, axis, [(i, i ^ turn) for i in range(size)])]
    broadcast_in_dim x1 -> x0, local copies, waits for them, and re-layouts: 47.5 us -> none  [shards(): spectra[None]]
    all_to_all x1 -> x0, local copies, waits for them, and re-layouts: 36 us -> none  [shards(): lax.all_to_all(spectra[None], ('stn', 'tm'), split_axis=1, concat_axis=0,...]
    unnamed x1 -> x0, other arithmetic: 35.9 us -> none
    ppermute x0 -> x15, starting transfers between devices: none -> 22 us  [swapped_with_each(): lax.ppermute(sent, axis, [(i, i ^ turn) for i in range(size)])]
    another operation x0 -> x3, local copies, waits for them, and re-layouts: none -> 20.8 us  [the longest x2 20.1 us: shards(): moved.reshape(stations, halves, per_dev, 2, inputs_dev, sub_count, spec_dev)]
    unnamed x9 -> x20, local copies, waits for them, and re-layouts: 28 us -> 10.8 us
  transfers between devices with their start and end apart: 1 -> 16, of which waited for: 1 -> 11; matrix products, arithmetic and copies ran while one was open for 0% -> 3% of each run, Pallas kernels for 0% -> 0%
where the time goes in v1:
time: 396 us; the launch traced here: 394 us
  waiting for transfers between devices  129 us (33%)
  other arithmetic  123 us (31%)
  local copies, waits for them, and re-layouts  83.8 us (21%)
  matrix products  35.7 us (9%)
  starting transfers between devices  22.1 us (6%)
    ppermute x15, waiting for transfers between devices, swapped_with_each(): lax.ppermute(sent, axis, [(i, i ^ turn) for i in range(size)])  127 us
    add x1, other arithmetic, shards(): filtered + filter_taps[tap_index] * extended[:, :, tap_index:tap_index +...  74.6 us
    mul x1, other arithmetic, shards(): return result * scale  23.2 us
    ppermute x15, starting transfers between devices, swapped_with_each(): lax.ppermute(sent, axis, [(i, i ^ turn) for i in range(size)])  22 us
    another operation x2, local copies, waits for them, and re-layouts, shards(): moved.reshape(stations, halves, per_dev, 2, inputs_dev, sub_count, spec_dev)  20.1 us
    dot_general x1, matrix products, correlate(): jnp.einsum('gcis,gcjs->gcij', left_imag, right_side, preferred_element_ty...  14.1 us
    dot_general x1, matrix products, shards(): lax.dot_general(table, filtered.reshape(-1, frame_len), (((0,), (1,)), ((...  13.1 us
    unnamed x20, local copies, waits for them, and re-layouts  10.8 us
  transfers between devices with their start and end apart: 16, of which 11 were waited for; matrix products, arithmetic and copies ran while one was open for 3% of the time, Pallas kernels for 0%

profile of v1, /device:TPU:1, one launch (start us, length us, event | category | flops | bytes accessed | tf_op | source)
XLA Modules:
  0.0 393.8 jit_solution(11022148168677715255)
XLA Ops:
  0.0 9.0 %convert_element_type.26 = bf16[88,2,16384]{2,1,0:T(2,128)(2,1)} convert(s32[88,2,16384]{2,1,0:T(2,128)} %param.2) | non-fusion elementwise | flops 2883584 | bytes 17301504 | tf_op jit(solution)/shard_map/convert_element_type | solution.py:76
  9.0 10.5 %reshape.173 = bf16[88,2,128,128]{3,2,1,0:T(8,128)(2,1)} reshape(bf16[88,2,16384]{2,1,0:T(2,128)(2,1)} %convert_element_type.26) | data formatting | bytes 11534336 | tf_op jit(solution)/shard_map/reshape | solution.py:76
  19.5 1.4 slice.148
  21.8 1.6 collective-permute-done
  23.7 10.6 %maximum_convert_fusion = f32[88,2,143,128]{3,2,0,1:T(8,128)} fusion(bf16[88,2,15,128]{3,2,0,1:T(8,128)(2,1)S(1)} %pad_select_fusion, bf16[88,2,128,128]{3,2,1,0:T(8,128)(2,1)} %reshape.173), kind=kLoop, calls=%fused_computation.37 | loop fusion | flops 12886016 | bytes 19329024 | tf_op jit(solution)/shard_map/convert_element_type | solution.py:81
  34.3 74.6 %fusion.1 = f32[88,2,128,128]{3,2,0,1:T(8,128)} fusion(f32[88,2,143,128]{3,2,0,1:T(8,128)} %maximum_convert_fusion, f32[128]{0:T(128)S(1)} %get-tuple-element.39, f32[128]{0:T(128)S(1)} %get-tuple-element.40, f32[128]{0:T(128)S(1)} %get-tuple-element.26, f32[128]{0:T(128)S(1)} %get-tuple-element.27, f32[128]{0:T(128)S(1)} %get-tuple-element.28, ...), kind=kLoop, calls=%fused_computation.5 | loop fusion | flops 89391104 | bytes 196091904 | tf_op jit(solution)/shard_map/add | solution.py:85
  108.9 10.6 %copy.17 = f32[88,2,128,128]{3,2,1,0:T(8,128)} copy(f32[88,2,128,128]{3,2,0,1:T(8,128)} %fusion.1) | data formatting | bytes 23068672 | tf_op jit(solution)/shard_map/add | solution.py:85
  119.6 13.1 %fusion = bf16[16,1,8,22528]{3,2,0,1:T(8,128)(2,1)S(1)} fusion(f32[128,128]{0,1:T(8,128)S(1)} %bitcast.113, f32[22528,128]{1,0:T(8,128)} %bitcast.111), kind=kOutput, calls=%fused_computation.3 | convolution fusion | flops 4432068608 | bytes 17367040 | tf_op jit(solution)/shard_map/dot_general | solution.py:88
  132.7 1.5 dynamic-slice_bitcast_fusion
  134.4 5.7 %collective-permute-start.15 = (bf16[1,8,22528]{2,1,0:T(8,128)(2,1)S(1)}, bf16[1,8,22528]{2,1,0:T(8,128)(2,1)S(1)}, u32[]{:S(2)}, u32[]{:S(2)}) collective-permute-start(bf16[1,8,22528]{2,1,0:T(8,128)(2,1)S(1)} %get-tuple-element.7), channel_id=1, source_target_pairs={{0,15},{1,14},{2,13},{3,12},{4,11},{5,10},{6,9},{7,8},{8,7},{9,6},... | collective-permute-start | bytes 1081352 | tf_op jit(solution)/shard_map/ppermute | solution.py:26
  140.1 3.7 collective-permute-start.13
  143.8 1.2 collective-permute-start.2
  145.8 18.7 %collective-permute-done.2 = bf16[1,8,22528]{2,1,0:T(8,128)(2,1)S(1)} collective-permute-done((bf16[1,8,22528]{2,1,0:T(8,128)(2,1)S(1)}, bf16[1,8,22528]{2,1,0:T(8,128)(2,1)S(1)}, u32[]{:S(2)}, u32[]{:S(2)}) %collective-permute-start.2) | collective-permute-done | bytes 360480 | tf_op jit(solution)/shard_map/ppermute | solution.py:26
  164.5 1.5 collective-permute-start.3
  166.8 8.3 %collective-permute-done.3 = bf16[1,8,22528]{2,1,0:T(8,128)(2,1)S(1)} collective-permute-done((bf16[1,8,22528]{2,1,0:T(8,128)(2,1)S(1)}, bf16[1,8,22528]{2,1,0:T(8,128)(2,1)S(1)}, u32[]{:S(2)}, u32[]{:S(2)}) %collective-permute-start.3) | collective-permute-done | bytes 360480 | tf_op jit(solution)/shard_map/ppermute | solution.py:26
  175.1 0.8 bitcast_dynamic-update-slice_fusion.12
  175.9 8.8 %collective-permute-done.4 = bf16[1,8,22528]{2,1,0:T(8,128)(2,1)S(1)} collective-permute-done((bf16[1,8,22528]{2,1,0:T(8,128)(2,1)S(1)}, bf16[1,8,22528]{2,1,0:T(8,128)(2,1)S(1)}, u32[]{:S(2)}, u32[]{:S(2)}) %collective-permute-start.4) | collective-permute-done | bytes 360480 | tf_op jit(solution)/shard_map/ppermute | solution.py:26
  184.7 1.1 collective-permute-start.5
  185.8 0.8 bitcast_dynamic-update-slice_fusion.11
  186.6 8.7 %collective-permute-done.5 = bf16[1,8,22528]{2,1,0:T(8,128)(2,1)S(1)} collective-permute-done((bf16[1,8,22528]{2,1,0:T(8,128)(2,1)S(1)}, bf16[1,8,22528]{2,1,0:T(8,128)(2,1)S(1)}, u32[]{:S(2)}, u32[]{:S(2)}) %collective-permute-start.5) | collective-permute-done | bytes 360480 | tf_op jit(solution)/shard_map/ppermute | solution.py:26
  195.2 1.9 collective-permute-start.6
  197.1 0.8 bitcast_dynamic-update-slice_fusion.10
  197.9 7.3 %collective-permute-done.6 = bf16[1,8,22528]{2,1,0:T(8,128)(2,1)S(1)} collective-permute-done((bf16[1,8,22528]{2,1,0:T(8,128)(2,1)S(1)}, bf16[1,8,22528]{2,1,0:T(8,128)(2,1)S(1)}, u32[]{:S(2)}, u32[]{:S(2)}) %collective-permute-start.6) | collective-permute-done | bytes 360480 | tf_op jit(solution)/shard_map/ppermute | solution.py:26
  205.2 3.6 collective-permute-start.7
  209.5 8.3 %collective-permute-done.7 = bf16[1,8,22528]{2,1,0:T(8,128)(2,1)S(1)} collective-permute-done((bf16[1,8,22528]{2,1,0:T(8,128)(2,1)S(1)}, bf16[1,8,22528]{2,1,0:T(8,128)(2,1)S(1)}, u32[]{:S(2)}, u32[]{:S(2)}) %collective-permute-start.7) | collective-permute-done | bytes 360480 | tf_op jit(solution)/shard_map/ppermute | solution.py:26
  217.9 3.0 collective-permute-start.8
  221.6 15.5 %collective-permute-done.8 = bf16[1,8,22528]{2,1,0:T(8,128)(2,1)S(1)} collective-permute-done((bf16[1,8,22528]{2,1,0:T(8,128)(2,1)S(1)}, bf16[1,8,22528]{2,1,0:T(8,128)(2,1)S(1)}, u32[]{:S(2)}, u32[]{:S(2)}) %collective-permute-start.8) | collective-permute-done | bytes 360480 | tf_op jit(solution)/shard_map/ppermute | solution.py:26
  237.2 0.8 bitcast_dynamic-update-slice_fusion.7
  237.9 18.6 %collective-permute-done.9 = bf16[1,8,22528]{2,1,0:T(8,128)(2,1)S(1)} collective-permute-done((bf16[1,8,22528]{2,1,0:T(8,128)(2,1)S(1)}, bf16[1,8,22528]{2,1,0:T(8,128)(2,1)S(1)}, u32[]{:S(2)}, u32[]{:S(2)}) %collective-permute-start.9) | collective-permute-done | bytes 360480 | tf_op jit(solution)/shard_map/ppermute | solution.py:26
  256.5 0.8 bitcast_dynamic-update-slice_fusion.6
  257.3 16.6 %collective-permute-done.10 = bf16[1,8,22528]{2,1,0:T(8,128)(2,1)S(1)} collective-permute-done((bf16[1,8,22528]{2,1,0:T(8,128)(2,1)S(1)}, bf16[1,8,22528]{2,1,0:T(8,128)(2,1)S(1)}, u32[]{:S(2)}, u32[]{:S(2)}) %collective-permute-start.10) | collective-permute-done | bytes 360480 | tf_op jit(solution)/shard_map/ppermute | solution.py:26
  273.9 0.8 bitcast_dynamic-update-slice_fusion.5
  274.7 16.6 %collective-permute-done.11 = bf16[1,8,22528]{2,1,0:T(8,128)(2,1)S(1)} collective-permute-done((bf16[1,8,22528]{2,1,0:T(8,128)(2,1)S(1)}, bf16[1,8,22528]{2,1,0:T(8,128)(2,1)S(1)}, u32[]{:S(2)}, u32[]{:S(2)}) %collective-permute-start.11) | collective-permute-done | bytes 360480 | tf_op jit(solution)/shard_map/ppermute | solution.py:26
  291.3 0.8 bitcast_dynamic-update-slice_fusion.4
  292.1 0.8 bitcast_dynamic-update-slice_fusion.3
  292.8 0.8 bitcast_dynamic-update-slice_fusion.2
  293.6 0.8 bitcast_dynamic-update-slice_fusion.1
  294.4 0.8 bitcast_dynamic-update-slice_fusion
  295.1 6.0 %gather_fusion = bf16[16,8,22528]{2,1,0:T(8,128)(2,1)} fusion(bf16[16,8,22528]{2,1,0:T(8,128)(2,1)} %bitcast.49, s32[1024]{0:T(1024)S(1)} %pad_clamp_fusion), kind=kCustom, calls=%fused_computation | custom fusion | bytes 11534400 | tf_op jit(solution)/shard_map/gather | solution.py:27
  301.2 8.9 %reshape_reshape.3 = bf16[8,2,4,2,88,2,128]{6,5,4,3,2,1,0:T(2,128)(2,1)} reshape(bf16[16,8,22528]{2,1,0:T(8,128)(2,1)} %gather_fusion) | data formatting | bytes 11534336 | tf_op jit(solution)/shard_map/reshape;reshape | solution.py:100
  310.1 11.2 %copy.25 = bf16[8,2,4,2,88,2,128]{6,1,4,0,2,5,3:T(2,128)(2,1)S(1)} copy(bf16[8,2,4,2,88,2,128]{6,5,4,3,2,1,0:T(2,128)(2,1)} %reshape_reshape.3) | data formatting | bytes 11534336 | tf_op jit(solution)/shard_map/reshape;reshape | solution.py:100
  321.3 7.7 %fusion.27 = (bf16[1,2,4,8,88,2,128]{6,5,4,3,2,1,0:T(2,128)(2,1)}, bf16[1,2,4,8,88,2,128]{6,5,4,3,2,1,0:T(2,128)(2,1)}) fusion(bf16[2,2,4,8,88,2,128]{6,5,4,3,2,1,0:T(2,128)(2,1)S(1)} %bitcast.112), kind=kLoop, calls=%fused_computation.109 | loop fusion | bytes 11534336 | tf_op jit(solution)/shard_map/slice | solution.py:58
  329.0 6.4 %squeeze.67 = bf16[2,4,704,256]{3,2,1,0:T(8,128)(2,1)S(1)} reshape(bf16[1,2,4,8,88,2,128]{6,5,4,3,2,1,0:T(2,128)(2,1)} %get-tuple-element.5) | data formatting | bytes 5767168 | tf_op jit(solution)/shard_map/squeeze | solution.py:58
  335.3 7.4 %squeeze.66 = bf16[2,4,704,256]{3,2,1,0:T(8,128)(2,1)} reshape(bf16[1,2,4,8,88,2,128]{6,5,4,3,2,1,0:T(2,128)(2,1)} %get-tuple-element.6) | data formatting | bytes 5767168 | tf_op jit(solution)/shard_map/squeeze | solution.py:57
  342.8 5.0 %fusion.28 = (bf16[2,4,704,256]{3,2,1,0:T(8,128)(2,1)}, bf16[2,4,704,512]{3,2,1,0:T(8,128)(2,1)S(1)}) fusion(bf16[2,4,704,256]{3,2,1,0:T(8,128)(2,1)} %squeeze.66), kind=kLoop, calls=%fused_computation.110 | loop fusion | flops 4325375 | bytes 8650752 | tf_op jit(solution)/shard_map/neg | solution.py:60
  348.1 8.4 %convolution_bitcast_fusion.1 = f32[1,2,4,704,704]{4,3,2,1,0:T(8,128)} fusion(bf16[2,4,704,512]{3,2,1,0:T(8,128)(2,1)S(1)} %constant_dynamic-update-slice_fusion), kind=kOutput, calls=%fused_computation.36 | convolution fusion | flops 4060086272 | bytes 21626880 | tf_op jit(solution)/shard_map/gcis,gcjs->gcij/dot_general | solution.py:61
  356.5 14.1 %convolution_bitcast_fusion = f32[1,2,4,704,704]{4,3,2,1,0:T(8,128)} fusion(bf16[2,4,704,512]{3,2,1,0:T(8,128)(2,1)} %copy-done, bf16[2,4,704,256]{3,2,1,0:T(8,128)(2,1)} %get-tuple-element.23, bf16[2,4,704,256]{3,2,1,0:T(8,128)(2,1)S(1)} %squeeze.67), kind=kOutput, calls=%fused_computation.35 | convolution fusion | flops 4071620608 | bytes 27394048 | tf_op jit(solution)/shard_map/gcis,gcjs->gcij/dot_general | solution.py:64
  370.6 23.2 %maximum_multiply_fusion = f32[2,2,4,704,704]{4,3,2,1,0:T(8,128)} fusion(f32[1,2,4,704,704]{4,3,2,1,0:T(8,128)} %convolution_bitcast_fusion, f32[1,2,4,704,704]{4,3,2,1,0:T(8,128)} %convolution_bitcast_fusion.1), kind=kLoop, calls=%fused_computation.1 | loop fusion | flops 15859712 | bytes 63438848 | tf_op jit(solution)/shard_map/mul | solution.py:102
  (34 shorter events, 4.5 us)
Async XLA Ops:
  9.0 12.8 %copy-start.1 = (f32[16,128]{1,0:T(8,128)S(1)}, f32[16,128]{1,0:T(8,128)}, u32[]{:S(2)}) copy-start(f32[16,128]{1,0:T(8,128)} %param.3) | copy-start | bytes 24580
  21.2 2.2 collective-permute-start
  134.2 9.6 %collective-permute-start.1 = (bf16[1,8,22528]{2,1,0:T(8,128)(2,1)S(1)}, bf16[1,8,22528]{2,1,0:T(8,128)(2,1)S(1)}, u32[]{:S(2)}, u32[]{:S(2)}) collective-permute-start(bf16[1,8,22528]{2,1,0:T(8,128)(2,1)S(1)} %get-tuple-element.21), channel_id=1, source_target_pairs={{0,1},{1,0},{2,3},{3,2},{4,5},{5,4},{6,7},{7,6},{8,9},{9,8},{10,11... | collective-permute-start | bytes 1081352 | tf_op jit(solution)/shard_map/ppermute | solution.py:26
  134.4 160.0 %collective-permute-start.15 = (bf16[1,8,22528]{2,1,0:T(8,128)(2,1)S(1)}, bf16[1,8,22528]{2,1,0:T(8,128)(2,1)S(1)}, u32[]{:S(2)}, u32[]{:S(2)}) collective-permute-start(bf16[1,8,22528]{2,1,0:T(8,128)(2,1)S(1)} %get-tuple-element.7), channel_id=1, source_target_pairs={{0,15},{1,14},{2,13},{3,12},{4,11},{5,10},{6,9},{7,8},{8,7},{9,6},... | collective-permute-start | bytes 1081352 | tf_op jit(solution)/shard_map/ppermute | solution.py:26
  140.1 153.5 %collective-permute-start.14 = (bf16[1,8,22528]{2,1,0:T(8,128)(2,1)S(1)}, bf16[1,8,22528]{2,1,0:T(8,128)(2,1)S(1)}, u32[]{:S(2)}, u32[]{:S(2)}) collective-permute-start(bf16[1,8,22528]{2,1,0:T(8,128)(2,1)S(1)} %get-tuple-element.8), channel_id=1, source_target_pairs={{0,14},{1,15},{2,12},{3,13},{4,10},{5,11},{6,8},{7,9},{8,6},{9,7},... | collective-permute-start | bytes 1081352 | tf_op jit(solution)/shard_map/ppermute | solution.py:26
  140.1 152.7 %collective-permute-start.13 = (bf16[1,8,22528]{2,1,0:T(8,128)(2,1)S(1)}, bf16[1,8,22528]{2,1,0:T(8,128)(2,1)S(1)}, u32[]{:S(2)}, u32[]{:S(2)}) collective-permute-start(bf16[1,8,22528]{2,1,0:T(8,128)(2,1)S(1)} %get-tuple-element.9), channel_id=1, source_target_pairs={{0,13},{1,12},{2,15},{3,14},{4,9},{5,8},{6,11},{7,10},{8,5},{9,4},... | collective-permute-start | bytes 1081352 | tf_op jit(solution)/shard_map/ppermute | solution.py:26
  143.8 148.2 %collective-permute-start.12 = (bf16[1,8,22528]{2,1,0:T(8,128)(2,1)S(1)}, bf16[1,8,22528]{2,1,0:T(8,128)(2,1)S(1)}, u32[]{:S(2)}, u32[]{:S(2)}) collective-permute-start(bf16[1,8,22528]{2,1,0:T(8,128)(2,1)S(1)} %get-tuple-element.10), channel_id=1, source_target_pairs={{0,12},{1,13},{2,14},{3,15},{4,8},{5,9},{6,10},{7,11},{8,4},{9,5},... | collective-permute-start | bytes 1081352 | tf_op jit(solution)/shard_map/ppermute | solution.py:26
  143.8 20.7 %collective-permute-start.2 = (bf16[1,8,22528]{2,1,0:T(8,128)(2,1)S(1)}, bf16[1,8,22528]{2,1,0:T(8,128)(2,1)S(1)}, u32[]{:S(2)}, u32[]{:S(2)}) collective-permute-start(bf16[1,8,22528]{2,1,0:T(8,128)(2,1)S(1)} %get-tuple-element.20), channel_id=1, source_target_pairs={{0,2},{1,3},{2,0},{3,1},{4,6},{5,7},{6,4},{7,5},{8,10},{9,11},{10,... | collective-permute-start | bytes 1081352 | tf_op jit(solution)/shard_map/ppermute | solution.py:26
  164.5 10.6 %collective-permute-start.3 = (bf16[1,8,22528]{2,1,0:T(8,128)(2,1)S(1)}, bf16[1,8,22528]{2,1,0:T(8,128)(2,1)S(1)}, u32[]{:S(2)}, u32[]{:S(2)}) collective-permute-start(bf16[1,8,22528]{2,1,0:T(8,128)(2,1)S(1)} %get-tuple-element.19), channel_id=1, source_target_pairs={{0,3},{1,2},{2,1},{3,0},{4,7},{5,6},{6,5},{7,4},{8,11},{9,10},{10,... | collective-permute-start | bytes 1081352 | tf_op jit(solution)/shard_map/ppermute | solution.py:26
  175.1 9.6 %collective-permute-start.4 = (bf16[1,8,22528]{2,1,0:T(8,128)(2,1)S(1)}, bf16[1,8,22528]{2,1,0:T(8,128)(2,1)S(1)}, u32[]{:S(2)}, u32[]{:S(2)}) collective-permute-start(bf16[1,8,22528]{2,1,0:T(8,128)(2,1)S(1)} %get-tuple-element.18), channel_id=1, source_target_pairs={{0,4},{1,5},{2,6},{3,7},{4,0},{5,1},{6,2},{7,3},{8,12},{9,13},{10,... | collective-permute-start | bytes 1081352 | tf_op jit(solution)/shard_map/ppermute | solution.py:26
  184.7 10.5 %collective-permute-start.5 = (bf16[1,8,22528]{2,1,0:T(8,128)(2,1)S(1)}, bf16[1,8,22528]{2,1,0:T(8,128)(2,1)S(1)}, u32[]{:S(2)}, u32[]{:S(2)}) collective-permute-start(bf16[1,8,22528]{2,1,0:T(8,128)(2,1)S(1)} %get-tuple-element.17), channel_id=1, source_target_pairs={{0,5},{1,4},{2,7},{3,6},{4,1},{5,0},{6,3},{7,2},{8,13},{9,12},{10,... | collective-permute-start | bytes 1081352 | tf_op jit(solution)/shard_map/ppermute | solution.py:26
  195.2 10.0 %collective-permute-start.6 = (bf16[1,8,22528]{2,1,0:T(8,128)(2,1)S(1)}, bf16[1,8,22528]{2,1,0:T(8,128)(2,1)S(1)}, u32[]{:S(2)}, u32[]{:S(2)}) collective-permute-start(bf16[1,8,22528]{2,1,0:T(8,128)(2,1)S(1)} %get-tuple-element.16), channel_id=1, source_target_pairs={{0,6},{1,7},{2,4},{3,5},{4,2},{5,3},{6,0},{7,1},{8,14},{9,15},{10,... | collective-permute-start | bytes 1081352 | tf_op jit(solution)/shard_map/ppermute | solution.py:26
  205.2 12.7 %collective-permute-start.7 = (bf16[1,8,22528]{2,1,0:T(8,128)(2,1)S(1)}, bf16[1,8,22528]{2,1,0:T(8,128)(2,1)S(1)}, u32[]{:S(2)}, u32[]{:S(2)}) collective-permute-start(bf16[1,8,22528]{2,1,0:T(8,128)(2,1)S(1)} %get-tuple-element.15), channel_id=1, source_target_pairs={{0,7},{1,6},{2,5},{3,4},{4,3},{5,2},{6,1},{7,0},{8,15},{9,14},{10,... | collective-permute-start | bytes 1081352 | tf_op jit(solution)/shard_map/ppermute | solution.py:26
  217.9 19.3 %collective-permute-start.8 = (bf16[1,8,22528]{2,1,0:T(8,128)(2,1)S(1)}, bf16[1,8,22528]{2,1,0:T(8,128)(2,1)S(1)}, u32[]{:S(2)}, u32[]{:S(2)}) collective-permute-start(bf16[1,8,22528]{2,1,0:T(8,128)(2,1)S(1)} %get-tuple-element.14), channel_id=1, source_target_pairs={{0,8},{1,9},{2,10},{3,11},{4,12},{5,13},{6,14},{7,15},{8,0},{9,1},... | collective-permute-start | bytes 1081352 | tf_op jit(solution)/shard_map/ppermute | solution.py:26
  237.2 19.3 %collective-permute-start.9 = (bf16[1,8,22528]{2,1,0:T(8,128)(2,1)S(1)}, bf16[1,8,22528]{2,1,0:T(8,128)(2,1)S(1)}, u32[]{:S(2)}, u32[]{:S(2)}) collective-permute-start(bf16[1,8,22528]{2,1,0:T(8,128)(2,1)S(1)} %get-tuple-element.13), channel_id=1, source_target_pairs={{0,9},{1,8},{2,11},{3,10},{4,13},{5,12},{6,15},{7,14},{8,1},{9,0},... | collective-permute-start | bytes 1081352 | tf_op jit(solution)/shard_map/ppermute | solution.py:26
  256.5 17.4 %collective-permute-start.10 = (bf16[1,8,22528]{2,1,0:T(8,128)(2,1)S(1)}, bf16[1,8,22528]{2,1,0:T(8,128)(2,1)S(1)}, u32[]{:S(2)}, u32[]{:S(2)}) collective-permute-start(bf16[1,8,22528]{2,1,0:T(8,128)(2,1)S(1)} %get-tuple-element.12), channel_id=1, source_target_pairs={{0,10},{1,11},{2,8},{3,9},{4,14},{5,15},{6,12},{7,13},{8,2},{9,3},... | collective-permute-start | bytes 1081352 | tf_op jit(solution)/shard_map/ppermute | solution.py:26
  273.9 17.4 %collective-permute-start.11 = (bf16[1,8,22528]{2,1,0:T(8,128)(2,1)S(1)}, bf16[1,8,22528]{2,1,0:T(8,128)(2,1)S(1)}, u32[]{:S(2)}, u32[]{:S(2)}) collective-permute-start(bf16[1,8,22528]{2,1,0:T(8,128)(2,1)S(1)} %get-tuple-element.11), channel_id=1, source_target_pairs={{0,11},{1,10},{2,9},{3,8},{4,15},{5,14},{6,13},{7,12},{8,3},{9,2},... | collective-permute-start | bytes 1081352 | tf_op jit(solution)/shard_map/ppermute | solution.py:26
  348.1 8.4 %copy-start = (bf16[2,4,704,512]{3,2,1,0:T(8,128)(2,1)}, bf16[2,4,704,512]{3,2,1,0:T(8,128)(2,1)S(1)}, u32[]{:S(2)}) copy-start(bf16[2,4,704,512]{3,2,1,0:T(8,128)(2,1)S(1)} %constant_dynamic-update-slice_fusion) | copy-start | bytes 17301508
